TPU v7x, 32 devices: a whole 2x2x4 slice. The times are simulated.
32 devices in a mesh: dp: 2 (over x), ctx: 4 (over y, core), tp: 4 (over z).
Axes of the slice: x: 2, y: 2, z: 4, core: 2. Of those that a mesh axis runs over, the one named last changes fastest.
Arguments:
- tokens: bfloat16 [8192, 768], P(('dp', 'ctx')), may hold values from -6 to 6
- w_query: bfloat16 [768, 768], P('dp', 'tp'), may hold values from -0.3125 to 0.3125
- w_key: bfloat16 [768, 768], P('dp', 'tp'), may hold values from -0.3125 to 0.3125
- w_value: bfloat16 [768, 768], P('dp', 'tp'), may hold values from -0.21875 to 0.21875
- w_out: bfloat16 [768, 768], P('tp', 'dp'), may hold values from -1.75 to 1.75
- w_act: bfloat16 [768, 1152], P('dp', 'tp'), may hold values from -0.21875 to 0.21875
- w_up: bfloat16 [768, 1152], P('dp', 'tp'), may hold values from -0.21875 to 0.21875
- w_down: bfloat16 [1152, 768], P('tp', 'dp'), may hold values from -0.1875 to 0.1875
- gain_one: bfloat16 [768], P('dp'), may hold values from 0.5 to 1.5
- gain_two: bfloat16 [768], P('dp'), may hold values from 0.5 to 1.5
- cotangent: bfloat16 [8192, 768], P(('dp', 'ctx')), may hold values from -6 to 6
Outputs:
- outputs: bfloat16 [8192, 768], P(('dp', 'ctx', 'tp'))
- input_grad: bfloat16 [8192, 768], P(('dp', 'ctx', 'tp'))
- grad_query: float32 [768, 768], P('dp', 'tp')
- grad_key: float32 [768, 768], P('dp', 'tp')
- grad_value: float32 [768, 768], P('dp', 'tp')
- grad_out: float32 [768, 768], P('tp', 'dp')
- grad_act: float32 [768, 1152], P('dp', 'tp')
- grad_up: float32 [768, 1152], P('dp', 'tp')
- grad_down: float32 [1152, 768], P('tp', 'dp')
- grad_gain_one: float32 [768], P('dp')
- grad_gain_two: float32 [768], P('dp')
All inputs are finite; a program needn't handle non-finite values.
Results may differ from a plain program's by a relative error of at most 0.024.
Values may be sent and summed in bfloat16 or wider, within the bound.
A program may use at most 128 MiB of HBM per device.

v0:
```python
import math
import jax
import jax.numpy as jnp
from jax import lax
from jax.sharding import PartitionSpec as P

HEAD = 64
EPSILON = 1e-05
ROPE_BASE = 160000.0


def standardize(values_in):
    mean_value = jnp.mean(values_in, axis=-1, keepdims=True)
    centred = values_in - mean_value
    inverse = lax.rsqrt(jnp.mean(centred * centred, axis=-1, keepdims=True) + EPSILON)
    return (centred * inverse, inverse)


def norm_back(grad_hat, hat_values, inverse):
    mean_grad = jnp.mean(grad_hat, axis=-1, keepdims=True)
    mean_cross = jnp.mean(grad_hat * hat_values, axis=-1, keepdims=True)
    return inverse * (grad_hat - mean_grad - hat_values * mean_cross)


def rotate(tensor):
    half_size = tensor.shape[-1] // 2
    return jnp.concatenate([-tensor[..., half_size:], tensor[..., :half_size]], axis=-1)


def unrotate(tensor):
    half_size = tensor.shape[-1] // 2
    return jnp.concatenate([tensor[..., half_size:], -tensor[..., :half_size]], axis=-1)


def rotary(tensor, cosine_table, sine_table):
    return tensor * cosine_table + rotate(tensor) * sine_table


def rotary_back(tensor, cosine_table, sine_table):
    return tensor * cosine_table + unrotate(tensor * sine_table)


def tables(offset, length, head_size):
    position = (offset + jnp.arange(length)).astype(jnp.float32)
    frequency = ROPE_BASE ** (-jnp.arange(0, head_size, 2).astype(jnp.float32) / head_size)
    angles = position[:, None] * frequency[None, :]
    angles = jnp.concatenate([angles, angles], axis=1)
    return (jnp.cos(angles)[:, None, :], jnp.sin(angles)[:, None, :])


def gelu_parts(values_in):
    normal_cdf = 0.5 * (1.0 + lax.erf(values_in * (1.0 / math.sqrt(2.0))))
    density = jnp.exp(-0.5 * values_in * values_in) * (1.0 / math.sqrt(2.0 * math.pi))
    return (values_in * normal_cdf, normal_cdf + values_in * density)


def block_scores(query_block, key_block, factor):
    return (
        jnp.einsum("qhd,khd->hqk", query_block, key_block, preferred_element_type=jnp.float32)
        * factor
    )


def attend(queries, key_data, value_data, head_count):
    query_rows = queries.shape[0]
    key_rows = key_data.shape[0]
    query_step = math.gcd(query_rows, 512)
    factor = HEAD ** (-0.5)
    query_blocks = queries.reshape(query_rows // query_step, query_step, head_count, HEAD)
    key_all = key_data.reshape(key_rows, head_count, HEAD)
    value_all = value_data.reshape(key_rows, head_count, HEAD)

    def per_query(query_block):
        scores = block_scores(query_block, key_all, factor)
        log_total = jax.nn.logsumexp(scores, axis=-1)
        weights = jnp.exp(scores - log_total[:, :, None]).astype(jnp.bfloat16)
        accumulated = jnp.einsum(
            "hqk,khd->qhd", weights, value_all, preferred_element_type=jnp.float32
        )
        return (accumulated.reshape(query_step, head_count * HEAD), log_total.T)

    mixed_blocks, log_blocks = lax.map(per_query, query_blocks)
    return (
        mixed_blocks.reshape(query_rows, head_count * HEAD),
        log_blocks.reshape(query_rows, head_count),
    )


def attend_back(queries, grad_mixed, log_totals, totals, key_data, value_data, head_count):
    query_rows = queries.shape[0]
    key_rows = key_data.shape[0]
    query_step = math.gcd(query_rows, 512)
    key_step = math.gcd(key_rows, 1024)
    factor = HEAD ** (-0.5)
    query_blocks = queries.reshape(query_rows // query_step, query_step, head_count, HEAD)
    grad_blocks = grad_mixed.reshape(query_rows // query_step, query_step, head_count, HEAD)
    log_blocks = log_totals.reshape(query_rows // query_step, query_step, head_count)
    total_blocks = totals.reshape(query_rows // query_step, query_step, head_count)
    key_blocks = key_data.reshape(key_rows // key_step, key_step, head_count, HEAD)
    value_blocks = value_data.reshape(key_rows // key_step, key_step, head_count, HEAD)

    def per_query(running, block_item):
        key_accum, value_accum = running
        query_block, grad_block, log_block, total_block = block_item

        def per_key(query_accum, key_item):
            key_block, value_block, key_sum, value_sum = key_item
            scores = block_scores(query_block, key_block, factor)
            weights_full = jnp.exp(scores - log_block.T[:, :, None])
            value_sum = value_sum + jnp.einsum(
                "hqk,qhd->khd",
                weights_full.astype(jnp.bfloat16),
                grad_block,
                preferred_element_type=jnp.float32,
            )
            grad_probs = jnp.einsum(
                "qhd,khd->hqk", grad_block, value_block, preferred_element_type=jnp.float32
            )
            grad_scores = (factor * weights_full * (grad_probs - total_block.T[:, :, None])).astype(
                jnp.bfloat16
            )
            query_accum = query_accum + jnp.einsum(
                "hqk,khd->qhd", grad_scores, key_block, preferred_element_type=jnp.float32
            )
            key_sum = key_sum + jnp.einsum(
                "hqk,qhd->khd", grad_scores, query_block, preferred_element_type=jnp.float32
            )
            return (query_accum, (key_sum, value_sum))

        initial = jnp.zeros((query_step, head_count, HEAD), jnp.float32)
        query_accum, (key_accum, value_accum) = lax.scan(
            per_key, initial, (key_blocks, value_blocks, key_accum, value_accum)
        )
        return ((key_accum, value_accum), query_accum)

    zero_blocks = jnp.zeros(key_blocks.shape, jnp.float32)
    (key_accum, value_accum), query_accum = lax.scan(
        per_query, (zero_blocks, zero_blocks), (query_blocks, grad_blocks, log_blocks, total_blocks)
    )
    feature_count = head_count * HEAD
    return (
        query_accum.reshape(query_rows, feature_count),
        key_accum.reshape(key_rows, feature_count),
        value_accum.reshape(key_rows, feature_count),
    )


def owner_shares(
    query_grad,
    key_grad,
    value_grad,
    act_grad,
    up_grad,
    gain_first_grad,
    gain_second_grad,
    out_grad,
    down_grad,
):
    row_parts = (
        lax.psum_scatter(
            query_grad.astype(jnp.bfloat16), "dp", scatter_dimension=0, tiled=True
        ).astype(jnp.float32),
        lax.psum_scatter(
            key_grad.astype(jnp.bfloat16), "dp", scatter_dimension=0, tiled=True
        ).astype(jnp.float32),
        lax.psum_scatter(
            value_grad.astype(jnp.bfloat16), "dp", scatter_dimension=0, tiled=True
        ).astype(jnp.float32),
        lax.psum_scatter(
            act_grad.astype(jnp.bfloat16), "dp", scatter_dimension=0, tiled=True
        ).astype(jnp.float32),
        lax.psum_scatter(
            up_grad.astype(jnp.bfloat16), "dp", scatter_dimension=0, tiled=True
        ).astype(jnp.float32),
        lax.psum_scatter(
            gain_first_grad.astype(jnp.bfloat16), "dp", scatter_dimension=0, tiled=True
        ).astype(jnp.float32),
        lax.psum_scatter(
            gain_second_grad.astype(jnp.bfloat16), "dp", scatter_dimension=0, tiled=True
        ).astype(jnp.float32),
    )
    col_parts = (
        lax.psum_scatter(
            out_grad.astype(jnp.bfloat16), "dp", scatter_dimension=1, tiled=True
        ).astype(jnp.float32),
        lax.psum_scatter(
            down_grad.astype(jnp.bfloat16), "dp", scatter_dimension=1, tiled=True
        ).astype(jnp.float32),
    )
    return tuple(row_parts) + tuple(col_parts)


def context_total(query_grad, key_grad, value_grad, act_grad, up_grad, out_grad, down_grad):
    return tuple(
        (
            lax.psum(query_grad.astype(jnp.bfloat16), "ctx").astype(jnp.float32),
            lax.psum(key_grad.astype(jnp.bfloat16), "ctx").astype(jnp.float32),
            lax.psum(value_grad.astype(jnp.bfloat16), "ctx").astype(jnp.float32),
            lax.psum(act_grad.astype(jnp.bfloat16), "ctx").astype(jnp.float32),
            lax.psum(up_grad.astype(jnp.bfloat16), "ctx").astype(jnp.float32),
            lax.psum(out_grad.astype(jnp.bfloat16), "ctx").astype(jnp.float32),
            lax.psum(down_grad.astype(jnp.bfloat16), "ctx").astype(jnp.float32),
        )
    )


def local(
    tokens, w_query, w_key, w_value, w_out, w_act, w_up, w_down, gain_one, gain_two, cotangent
):
    tok_rows = tokens.shape[0]
    query_w, key_w, value_w, act_w, up_w, gain_first, gain_second = (
        lax.all_gather(w_query, "dp", axis=0, tiled=True),
        lax.all_gather(w_key, "dp", axis=0, tiled=True),
        lax.all_gather(w_value, "dp", axis=0, tiled=True),
        lax.all_gather(w_act, "dp", axis=0, tiled=True),
        lax.all_gather(w_up, "dp", axis=0, tiled=True),
        lax.all_gather(gain_one, "dp", axis=0, tiled=True),
        lax.all_gather(gain_two, "dp", axis=0, tiled=True),
    )
    out_w, down_w = (
        lax.all_gather(w_out, "dp", axis=1, tiled=True),
        lax.all_gather(w_down, "dp", axis=1, tiled=True),
    )
    head_count = query_w.shape[1] // HEAD
    feature_count = head_count * HEAD
    share_rows = tok_rows // lax.axis_size("tp")
    share_start = lax.axis_index("tp") * share_rows

    def own_rows(array_in):
        return lax.dynamic_slice_in_dim(array_in, share_start, share_rows, 0)

    cosine_table, sine_table = tables(lax.axis_index("ctx") * tok_rows, tok_rows, HEAD)
    gain_first_f = gain_first.astype(jnp.float32)
    gain_second_f = gain_second.astype(jnp.float32)
    inputs = tokens.astype(jnp.float32)
    hat_one, inverse_one = standardize(inputs)
    normed = (hat_one * gain_first_f).astype(jnp.bfloat16)
    query_pre = jnp.dot(normed, query_w, preferred_element_type=jnp.float32).reshape(
        tok_rows, head_count, HEAD
    )
    key_pre = jnp.dot(normed, key_w, preferred_element_type=jnp.float32).reshape(
        tok_rows, head_count, HEAD
    )
    queries = (
        rotary(query_pre, cosine_table, sine_table)
        .astype(jnp.bfloat16)
        .reshape(tok_rows, feature_count)
    )
    key_data = (
        rotary(key_pre, cosine_table, sine_table)
        .astype(jnp.bfloat16)
        .reshape(tok_rows, feature_count)
    )
    value_data = jnp.dot(normed, value_w, preferred_element_type=jnp.float32).astype(jnp.bfloat16)
    keys_all, values_all = (
        lax.all_gather(key_data, "ctx", axis=0, tiled=True),
        lax.all_gather(value_data, "ctx", axis=0, tiled=True),
    )
    mixed_full, log_totals = attend(
        queries.reshape(tok_rows, head_count, HEAD), keys_all, values_all, head_count
    )
    mixed_low = mixed_full.astype(jnp.bfloat16)
    middle = inputs + lax.psum(
        jnp.dot(mixed_low, out_w, preferred_element_type=jnp.float32).astype(jnp.bfloat16), "tp"
    ).astype(jnp.float32)
    hat_two, inverse_two = standardize(middle)
    normed_two = (hat_two * gain_second_f).astype(jnp.bfloat16)
    gate_in = jnp.dot(normed_two, act_w, preferred_element_type=jnp.float32)
    up_in = jnp.dot(normed_two, up_w, preferred_element_type=jnp.float32)
    active_in, derivative_in = gelu_parts(gate_in)
    hidden = (active_in * up_in).astype(jnp.bfloat16)
    outputs = middle + lax.psum(
        jnp.dot(hidden, down_w, preferred_element_type=jnp.float32).astype(jnp.bfloat16), "tp"
    ).astype(jnp.float32)
    out_rows = own_rows(outputs)
    grad_hidden = jnp.dot(cotangent, down_w.T, preferred_element_type=jnp.float32)
    grad_gate = (grad_hidden * up_in * derivative_in).astype(jnp.bfloat16)
    grad_upin = (grad_hidden * active_in).astype(jnp.bfloat16)
    down_grad = jnp.dot(hidden.T, cotangent, preferred_element_type=jnp.float32)
    act_grad = jnp.dot(normed_two.T, grad_gate, preferred_element_type=jnp.float32)
    up_grad = jnp.dot(normed_two.T, grad_upin, preferred_element_type=jnp.float32)
    grad_normed_two = lax.psum(
        (
            jnp.dot(grad_gate, act_w.T, preferred_element_type=jnp.float32)
            + jnp.dot(grad_upin, up_w.T, preferred_element_type=jnp.float32)
        ).astype(jnp.bfloat16),
        "tp",
    ).astype(jnp.float32)
    gain_second_grad = jnp.sum(own_rows(grad_normed_two) * own_rows(hat_two), axis=0)
    grad_middle = cotangent.astype(jnp.float32) + norm_back(
        grad_normed_two * gain_second_f, hat_two, inverse_two
    )
    grad_middle_low = grad_middle.astype(jnp.bfloat16)
    grad_middle_part = own_rows(grad_middle)
    out_grad = jnp.dot(mixed_low.T, grad_middle_low, preferred_element_type=jnp.float32)
    grad_mixed = jnp.dot(grad_middle_low, out_w.T, preferred_element_type=jnp.float32).astype(
        jnp.bfloat16
    )
    totals = jnp.sum(
        (grad_mixed.astype(jnp.float32) * mixed_full).reshape(tok_rows, head_count, HEAD), axis=-1
    )
    grad_qrot, key_part, value_part = attend_back(
        queries, grad_mixed, log_totals, totals, keys_all, values_all, head_count
    )
    grad_krot, grad_values = (
        lax.psum_scatter(
            key_part.astype(jnp.bfloat16), "ctx", scatter_dimension=0, tiled=True
        ).astype(jnp.float32),
        lax.psum_scatter(
            value_part.astype(jnp.bfloat16), "ctx", scatter_dimension=0, tiled=True
        ).astype(jnp.float32),
    )
    grad_q = (
        rotary_back(grad_qrot.reshape(tok_rows, head_count, HEAD), cosine_table, sine_table)
        .reshape(tok_rows, feature_count)
        .astype(jnp.bfloat16)
    )
    grad_k = (
        rotary_back(grad_krot.reshape(tok_rows, head_count, HEAD), cosine_table, sine_table)
        .reshape(tok_rows, feature_count)
        .astype(jnp.bfloat16)
    )
    grad_v = grad_values.astype(jnp.bfloat16)
    query_grad = jnp.dot(normed.T, grad_q, preferred_element_type=jnp.float32)
    key_grad = jnp.dot(normed.T, grad_k, preferred_element_type=jnp.float32)
    value_grad = jnp.dot(normed.T, grad_v, preferred_element_type=jnp.float32)
    grad_normed_part = own_rows(
        lax.psum(
            (
                jnp.dot(grad_q, query_w.T, preferred_element_type=jnp.float32)
                + jnp.dot(grad_k, key_w.T, preferred_element_type=jnp.float32)
                + jnp.dot(grad_v, value_w.T, preferred_element_type=jnp.float32)
            ).astype(jnp.bfloat16),
            "tp",
        ).astype(jnp.float32)
    )
    hat_one_part = own_rows(hat_one)
    gain_first_part = jnp.sum(grad_normed_part * hat_one_part, axis=0)
    input_rows = grad_middle_part + norm_back(
        grad_normed_part * gain_first_f, hat_one_part, own_rows(inverse_one)
    )
    gain_first_grad, gain_second_total = lax.psum(
        (gain_first_part, gain_second_grad), ("ctx", "tp")
    )
    summed = context_total(query_grad, key_grad, value_grad, act_grad, up_grad, out_grad, down_grad)
    shares = owner_shares(
        summed[0],
        summed[1],
        summed[2],
        summed[3],
        summed[4],
        gain_first_grad,
        gain_second_total,
        summed[5],
        summed[6],
    )
    return (
        out_rows.astype(jnp.bfloat16),
        input_rows.astype(jnp.bfloat16),
        shares[0],
        shares[1],
        shares[2],
        shares[7],
        shares[3],
        shares[4],
        shares[8],
        shares[5],
        shares[6],
    )


def solution(mesh):
    in_specs = (
        P(("dp", "ctx"), None),
        P("dp", "tp"),
        P("dp", "tp"),
        P("dp", "tp"),
        P("tp", "dp"),
        P("dp", "tp"),
        P("dp", "tp"),
        P("tp", "dp"),
        P("dp"),
        P("dp"),
        P(("dp", "ctx"), None),
    )
    out_specs = (
        P(("dp", "ctx", "tp"), None),
        P(("dp", "ctx", "tp"), None),
        P("dp", "tp"),
        P("dp", "tp"),
        P("dp", "tp"),
        P("tp", "dp"),
        P("dp", "tp"),
        P("dp", "tp"),
        P("tp", "dp"),
        P("dp"),
        P("dp"),
    )
    return jax.shard_map(local, mesh=mesh, in_specs=in_specs, out_specs=out_specs, check_vma=False)
```

profile of v0, /device:TPU:0, one launch (start us, length us, event | category | flops | bytes accessed | tf_op | source)
XLA Modules:
  0.0 796.8 jit_solution(9328104708917841218)
XLA Ops:
  8.1 5.2 all-gather
  17.1 5.8 all_gather.37
  26.6 5.8 all_gather.35
  35.4 5.8 all_gather.34
  48.6 6.3 all_gather.39
  54.8 15.1 %all-gather.5.cloned.1.call-done = bf16[4096,192]{0,1:T(8,128)(2,1)} async-done(((bf16[1024,192]{0,1:T(8,128)(2,1)}), bf16[4096,192]{0,1:T(8,128)(2,1)}) %all-gather.5.cloned.1.call-update) | async-done | bytes 1572880 | tf_op jit(solution)/shard_map/all_gather | solution.py:256
  69.9 58.7 %while.42 = (s32[]{:T(128)}, f32[2,512,192]{1,0,2:T(2,128)}, f32[2,512,3]{1,2,0:T(4,128)S(1)}, bf16[2,512,3,64]{1,3,2,0:T(8,128)(2,1)S(1)}, bf16[4096,3,64]{0,2,...) while((s32[]{:T(128)}, f32[2,512,192]{1,0,2:T(2,128)}, f32[2,512,3]{1,2,0:T(4,128)S(1)}, ...), condition=%wide.region_5.6_spmd, body=%wide.region_2.5_spmd.sunk | while | flops 1660956672 | bytes 194132176 | solution.py:82
  74.9 5.0 exponential_reduce_fusion.2
  83.8 10.6 %fusion.155 = f32[3,512,64]{1,2,0:T(8,128)S(1)} fusion(bf16[4096,3,64]{0,2,1:T(8,128)(2,1)S(1)} %copy-done.2, f32[3,512,4096]{2,1,0:T(8,128)} %copy-done, f32[3,512]{1,0:T(4,128)S(1)} %fusion.154), kind=kOutput, calls=%fused_computation.3.clone.1 | convolution fusion | flops 824180736 | bytes 27138048 | tf_op jit(solution)/shard_map/while/body/eval_jaxpr/hqk,khd->qhd/dot_general | solution.py:77
  99.3 5.0 multiply_reduce_fusion.6
  113.1 10.6 %fusion.155 = f32[3,512,64]{1,2,0:T(8,128)S(1)} fusion(bf16[4096,3,64]{0,2,1:T(8,128)(2,1)S(1)} %copy-done.2, f32[3,512,4096]{2,1,0:T(8,128)} %copy-done, f32[3,512]{1,0:T(4,128)S(1)} %fusion.154), kind=kOutput, calls=%fused_computation.3.clone.1 | convolution fusion | flops 824180736 | bytes 27138048 | tf_op jit(solution)/shard_map/while/body/eval_jaxpr/hqk,khd->qhd/dot_general | solution.py:77
  138.1 7.2 all_gather.41
  145.3 6.7 all_gather.42
  152.0 7.3 all_gather.43
  159.3 43.0 %all-reduce.11.cloned.1.call-done = bf16[1024,768]{1,0:T(8,128)(2,1)} async-done(((bf16[1024,768]{1,0:T(8,128)(2,1)}), bf16[1024,768]{1,0:T(8,128)(2,1)}) %all-reduce.11.cloned.1.call-update) | async-done | bytes 1572880 | tf_op jit(solution)/shard_map/psum | solution.py:263
  225.9 58.4 %all-reduce.13.cloned.1.call-done = bf16[1024,768]{1,0:T(8,128)(2,1)} async-done(((bf16[1024,768]{1,0:T(8,128)(2,1)}), bf16[1024,768]{1,0:T(8,128)(2,1)}) %all-reduce.13.cloned.1.call-update) | async-done | bytes 1572880 | tf_op jit(solution)/shard_map/psum | solution.py:282
  299.2 99.6 %while.44 = (s32[]{:T(128)}, f32[4,1024,3,64]{1,3,2,0:T(8,128)}, f32[4,1024,3,64]{1,3,2,0:T(8,128)}, f32[2,512,3,64]{1,0,3,2:T(2,128)}, bf16[2,512,3,64]{1,3,2,0...) while((s32[]{:T(128)}, f32[4,1024,3,64]{1,3,2,0:T(8,128)}, ...), condition=%wide.region_17.18_spmd, body=%wide.region_14.17_spmd.sunk | while | flops 1021378560 | bytes 39758236 | solution.py:137
  299.2 41.3 %while.45 = (s32[]{:T(128)}, f32[512,3,64]{0,2,1:T(8,128)S(1)}, f32[4,1024,3,64]{1,3,2,0:T(8,128)}, f32[4,1024,3,64]{1,3,2,0:T(8,128)}, bf16[4,1024,3,64]{1,3,2,...) while((s32[]{:T(128)}, f32[512,3,64]{0,2,1:T(8,128)S(1)}, ...), condition=%wide.region_16.16_spmd.clone.clone, body=%wide.region_15.15_spmd.clone.clone.sunk | while | flops 1021378560 | bytes 37374108 | solution.py:131
  340.9 8.1 %dynamic_update_slice.33 = f32[2,512,3,64]{1,0,3,2:T(2,128)} dynamic-update-slice(f32[2,512,3,64]{1,0,3,2:T(2,128)} %get-tuple-element.656, f32[1,512,3,64]{1,0,3,2:T(1,128)S(1)} %copy.87, s32[]{:T(128)S(6)} %copy.120, s32[]{:T(128)} %constant.57.clone.1..sunk.1, s32[]{:T(128)} %constant.57.clone.1..sunk.1, s32[]{:T(128)} %constant.57.clone.1..sunk.1) | dynamic-update-slice | bytes 786436 | tf_op jit(solution)/shard_map/while/body/jit(dynamic_update_index_in_dim)/dynamic_update_slice | solution.py:137
  349.0 41.3 %while.45 = (s32[]{:T(128)}, f32[512,3,64]{0,2,1:T(8,128)S(1)}, f32[4,1024,3,64]{1,3,2,0:T(8,128)}, f32[4,1024,3,64]{1,3,2,0:T(8,128)}, bf16[4,1024,3,64]{1,3,2,...) while((s32[]{:T(128)}, f32[512,3,64]{0,2,1:T(8,128)S(1)}, ...), condition=%wide.region_16.16_spmd.clone.clone, body=%wide.region_15.15_spmd.clone.clone.sunk | while | flops 1021378560 | bytes 37374108 | solution.py:131
  390.8 8.1 %dynamic_update_slice.33 = f32[2,512,3,64]{1,0,3,2:T(2,128)} dynamic-update-slice(f32[2,512,3,64]{1,0,3,2:T(2,128)} %get-tuple-element.656, f32[1,512,3,64]{1,0,3,2:T(1,128)S(1)} %copy.87, s32[]{:T(128)S(6)} %copy.120, s32[]{:T(128)} %constant.57.clone.1..sunk.1, s32[]{:T(128)} %constant.57.clone.1..sunk.1, s32[]{:T(128)} %constant.57.clone.1..sunk.1) | dynamic-update-slice | bytes 786436 | tf_op jit(solution)/shard_map/while/body/jit(dynamic_update_index_in_dim)/dynamic_update_slice | solution.py:137
  437.3 24.9 %reduce-scatter.26.cloned.1.call-done = bf16[1024,192]{0,1:T(8,128)(2,1)} async-done(((bf16[4096,192]{0,1:T(8,128)(2,1)}), bf16[1024,192]{0,1:T(8,128)(2,1)}) %reduce-scatter.26.cloned.1.call-update) | async-done | bytes 393232 | tf_op jit(solution)/shard_map/reduce_scatter | solution.py:309
  467.9 11.8 %reduce-scatter.40.cloned.1.call-done = bf16[384,288]{1,0:T(8,128)(2,1)} async-done(((bf16[768,288]{1,0:T(8,128)(2,1)}), bf16[384,288]{1,0:T(8,128)(2,1)}) %reduce-scatter.40.cloned.1.call-update) | async-done | bytes 221200
  481.5 15.9 %reduce-scatter.36.cloned.1.call-done = bf16[384,288]{1,0:T(8,128)(2,1)} async-done(((bf16[768,288]{1,0:T(8,128)(2,1)}), bf16[384,288]{1,0:T(8,128)(2,1)}) %reduce-scatter.36.cloned.1.call-update) | async-done | bytes 221200
  499.2 15.8 %reduce-scatter.38.cloned.1.call-done = bf16[384,288]{1,0:T(8,128)(2,1)} async-done(((bf16[768,288]{1,0:T(8,128)(2,1)}), bf16[384,288]{1,0:T(8,128)(2,1)}) %reduce-scatter.38.cloned.1.call-update) | async-done | bytes 221200
  516.8 14.1 %reduce-scatter.34.cloned.1.call-done = bf16[384,192]{1,0:T(8,128)(2,1)} async-done(((bf16[768,192]{1,0:T(8,128)(2,1)}), bf16[384,192]{1,0:T(8,128)(2,1)}) %reduce-scatter.34.cloned.1.call-update) | async-done | bytes 147472
  534.3 12.6 %reduce-scatter.30.cloned.1.call-done = bf16[384,192]{1,0:T(8,128)(2,1)} async-done(((bf16[768,192]{1,0:T(8,128)(2,1)}), bf16[384,192]{1,0:T(8,128)(2,1)}) %reduce-scatter.30.cloned.1.call-update) | async-done | bytes 147472
  548.6 14.2 %reduce-scatter.28.cloned.1.call-done = bf16[384,192]{1,0:T(8,128)(2,1)} async-done(((bf16[768,192]{1,0:T(8,128)(2,1)}), bf16[384,192]{1,0:T(8,128)(2,1)}) %reduce-scatter.28.cloned.1.call-update) | async-done | bytes 147472
  564.5 14.3 %reduce-scatter.32.cloned.1.call-done = bf16[384,192]{1,0:T(8,128)(2,1)} async-done(((bf16[768,192]{1,0:T(8,128)(2,1)}), bf16[384,192]{1,0:T(8,128)(2,1)}) %reduce-scatter.32.cloned.1.call-update) | async-done | bytes 147472
  588.4 33.7 %all-reduce.17.cloned.1.call-done = (bf16[384,192]{0,1:T(8,128)(2,1)}, bf16[384,192]{0,1:T(8,128)(2,1)}, bf16[384,192]{0,1:T(8,128)(2,1)}, bf16[192,384]{1,0:T(8...) async-done(((bf16[384,192]{0,1:T(8,128)(2,1)}, bf16[384,192]{0,1:T(8,128)(2,1)}, bf16[384,192]{0,1:T(8,128)(2,1)}, ...) | async-done | bytes 1253392 | tf_op jit(solution)/shard_map/psum | solution.py:196
  633.0 112.9 %all-reduce.15.cloned.1.call-done = (bf16[1024,768]{1,0:T(8,128)(2,1)}, bf16[1024,768]{1,0:T(8,128)(2,1)}) async-done(((bf16[1024,768]{1,0:T(8,128)(2,1)}, bf16[1024,768]{1,0:T(8,128)(2,1)}), (bf16[1024,768]{1,0:T(8,128)(2,1)}, bf16[1024,768]{1,0:T(8,128)(2,1)})) %all-reduce.15.cloned.1.call-update) | async-done | bytes 3145744 | tf_op jit(solution)/shard_map/psum | solution.py:272
  747.1 32.3 %all-reduce.2 = (bf16[768]{0:T(1024)(128)(2,1)S(1)}, bf16[768]{0:T(1024)(128)(2,1)S(1)}) all-reduce(f32[768]{0:T(1024)S(1)} %get-tuple-element.271, f32[768]{0:T(1024)S(1)} %multiply_reduce_fusion.4), channel_id=1, replica_groups=mesh['dp'=2,'ctx'=4,'tp'=4] {'ctx','tp'}, use_global_device_ids=true, to_apply=%region_38.39 | all-reduce | flops 1536 | bytes 9216 | tf_op jit(solution)/shard_map/psum | solution.py:342
  (343 shorter events, 264.3 us)
Async XLA Ops:
  7.2 15.7 %copy-start.4 = (bf16[1024,768]{1,0:T(8,128)(2,1)S(1)}, bf16[1024,768]{1,0:T(8,128)(2,1)}, u32[]{:S(2)}) copy-start(bf16[1024,768]{1,0:T(8,128)(2,1)} %param.17) | copy-start | bytes 4718596
  7.2 9.8 %copy-start.46 = (bf16[384,192]{0,1:T(8,128)(2,1)S(1)}, bf16[384,192]{0,1:T(8,128)(2,1)}, u32[]{:S(2)}) copy-start(bf16[384,192]{0,1:T(8,128)(2,1)} %param.20) | copy-start | bytes 442372
  7.2 47.6 %all-gather.7.cloned.1.call-start = ((), (), s32[]{:S(2)}) async-start(), calls=%async_computation.10 | async-start | bytes 1966080 | tf_op jit(solution)/shard_map/all_gather | solution.py:257
  13.3 11.8 %copy-start.50 = (f32[768]{0:T(1024)}, f32[768]{0:T(1024)S(1)}, u32[]{:S(2)}) copy-start(f32[768]{0:T(1024)S(1)} %reshape.248) | copy-start | bytes 9220
  25.1 16.1 %copy-start.6 = (bf16[1024,768]{1,0:T(8,128)(2,1)}, bf16[1024,768]{1,0:T(8,128)(2,1)S(1)}, u32[]{:S(2)}) copy-start(bf16[1024,768]{1,0:T(8,128)(2,1)S(1)} %get-tuple-element.356) | copy-start | bytes 4718596
  26.5 43.4 %all-gather.5.cloned.1.call-start = ((), (), s32[]{:S(2)}) async-start(), calls=%async_computation.9 | async-start | bytes 1966080 | tf_op jit(solution)/shard_map/all_gather | solution.py:256
  35.3 167.1 %all-reduce.11.cloned.1.call-start = ((), (), s32[]{:S(2)}) async-start(), calls=%async_computation.11 | async-start | bytes 3145728 | tf_op jit(solution)/shard_map/psum | solution.py:263
  74.9 8.9 %copy-start = (f32[3,512,4096]{2,1,0:T(8,128)}, f32[3,512,4096]{2,1,0:T(8,128)S(1)}, u32[]{:S(2)}) copy-start(f32[3,512,4096]{2,1,0:T(8,128)S(1)} %get-tuple-element.547) | copy-start | bytes 75497472 | tf_op jit(solution)/shard_map/while
  83.8 11.1 %copy-start.36 = (f32[2,512,192]{1,0,2:T(2,128)S(1)}, f32[2,512,192]{1,0,2:T(2,128)}, u32[]{:S(2)}) copy-start(f32[2,512,192]{1,0,2:T(2,128)} %get-tuple-element.624) | copy-start | bytes 2359300 | tf_op jit(solution)/shard_map/while
  113.1 11.1 %copy-start.36 = (f32[2,512,192]{1,0,2:T(2,128)S(1)}, f32[2,512,192]{1,0,2:T(2,128)}, u32[]{:S(2)}) copy-start(f32[2,512,192]{1,0,2:T(2,128)} %get-tuple-element.624) | copy-start | bytes 2359300 | tf_op jit(solution)/shard_map/while
  128.6 9.5 %copy-start.42 = (bf16[384,288]{0,1:T(8,128)(2,1)S(1)}, bf16[384,288]{0,1:T(8,128)(2,1)}, u32[]{:S(2)}) copy-start(bf16[384,288]{0,1:T(8,128)(2,1)} %param.22) | copy-start | bytes 663556
  128.6 16.7 %copy-start.43 = (bf16[384,288]{0,1:T(8,128)(2,1)S(1)}, bf16[384,288]{0,1:T(8,128)(2,1)}, u32[]{:S(2)}) copy-start(bf16[384,288]{0,1:T(8,128)(2,1)} %param.23) | copy-start | bytes 663556
  129.9 74.4 %copy-start.17 = (f32[24,8,2,512]{3,1,2,0:T(8,128)}, f32[24,8,2,512]{3,1,2,0:T(8,128)S(1)}, u32[]{:S(2)}) copy-start(f32[24,8,2,512]{3,1,2,0:T(8,128)S(1)} %copy.80) | copy-start | bytes 2359300
  129.9 22.1 %copy-start.44 = (bf16[288,384]{1,0:T(8,128)(2,1)S(1)}, bf16[288,384]{1,0:T(8,128)(2,1)}, u32[]{:S(2)}) copy-start(bf16[288,384]{1,0:T(8,128)(2,1)} %param.24) | copy-start | bytes 663556
  130.0 72.4 %copy-start.5 = (bf16[1024,768]{1,0:T(8,128)(2,1)S(1)}, bf16[1024,768]{1,0:T(8,128)(2,1)}, u32[]{:S(2)}) copy-start(bf16[1024,768]{1,0:T(8,128)(2,1)} %param.17) | copy-start | bytes 4718596
  133.1 151.2 %all-reduce.13.cloned.1.call-start = ((), (), s32[]{:S(2)}) async-start(), calls=%async_computation.12 | async-start | bytes 3145728 | tf_op jit(solution)/shard_map/psum | solution.py:282
  215.9 215.5 %reduce-scatter.24.cloned.1.call-start = ((), (), s32[]{:S(2)}) async-start(), calls=%async_computation.13 | async-start | bytes 1966080 | tf_op jit(solution)/shard_map/reduce_scatter | solution.py:306
  404.1 58.1 %reduce-scatter.26.cloned.1.call-start = ((), (), s32[]{:S(2)}) async-start(), calls=%async_computation.14 | async-start | bytes 1966080 | tf_op jit(solution)/shard_map/reduce_scatter | solution.py:309
  407.9 71.8 %reduce-scatter.40.cloned.1.call-start = ((), (), s32[]{:S(2)}) async-start(), calls=%async_computation.21 | async-start | bytes 884736
  412.7 84.7 %reduce-scatter.36.cloned.1.call-start = ((), (), s32[]{:S(2)}) async-start(), calls=%async_computation.19 | async-start | bytes 884736
  415.6 99.4 %reduce-scatter.38.cloned.1.call-start = ((), (), s32[]{:S(2)}) async-start(), calls=%async_computation.20 | async-start | bytes 884736
  420.9 110.0 %reduce-scatter.34.cloned.1.call-start = ((), (), s32[]{:S(2)}) async-start(), calls=%async_computation.18 | async-start | bytes 589824
  422.6 8.9 %copy-start.27 = (f32[1024,64]{0,1:T(8,128)S(1)}, f32[1024,64]{0,1:T(8,128)}, u32[]{:S(2)}) copy-start(f32[1024,64]{0,1:T(8,128)} %copy-done.26) | copy-start | bytes 786436
  426.6 120.3 %reduce-scatter.30.cloned.1.call-start = ((), (), s32[]{:S(2)}) async-start(), calls=%async_computation.16 | async-start | bytes 589824
  435.8 127.0 %reduce-scatter.28.cloned.1.call-start = ((), (), s32[]{:S(2)}) async-start(), calls=%async_computation.15 | async-start | bytes 589824
  435.8 28.9 %copy-start.41 = (bf16[288,768]{1,0:T(8,128)(2,1)S(1)}, bf16[288,768]{1,0:T(8,128)(2,1)}, u32[]{:S(2)}) copy-start(bf16[288,768]{1,0:T(8,128)(2,1)} %all_gather.43) | copy-start | bytes 1327108
  437.3 141.5 %reduce-scatter.32.cloned.1.call-start = ((), (), s32[]{:S(2)}) async-start(), calls=%async_computation.17 | async-start | bytes 589824
  464.6 157.5 %all-reduce.17.cloned.1.call-start = ((), (), s32[]{:S(2)}) async-start(), calls=%async_computation.23 | async-start | bytes 2506752 | tf_op jit(solution)/shard_map/psum | solution.py:196
  580.5 165.3 %all-reduce.15.cloned.1.call-start = ((), (), s32[]{:S(2)}) async-start(), calls=%async_computation.22 | async-start | bytes 6291456 | tf_op jit(solution)/shard_map/psum | solution.py:272
  586.8 159.0 %copy-start.19 = (f32[1024,768]{1,0:T(8,128)S(1)}, f32[1024,768]{1,0:T(8,128)}, u32[]{:S(2)}) copy-start(f32[1024,768]{1,0:T(8,128)} %get-tuple-element.355) | copy-start | bytes 9437188
  586.8 159.0 %copy-start.51 = (f32[768]{0:T(1024)S(1)}, f32[768]{0:T(1024)}, u32[]{:S(2)}) copy-start(f32[768]{0:T(1024)} %copy-done.50) | copy-start | bytes 9220
  622.1 10.1 %copy-start.45 = (bf16[288,384]{1,0:T(8,128)(2,1)S(1)}, bf16[288,384]{1,0:T(8,128)(2,1)}, u32[]{:S(2)}) copy-start(bf16[288,384]{1,0:T(8,128)(2,1)} %get-tuple-element.338) | copy-start | bytes 663556
  (46 other events, 137.7 us)
Sparse Core Ops, SparseCore 0:
  26.6 21.4 all-gather.6
  50.2 19.6 all-gather.4
  133.2 69.0 all-reduce.10
  216.1 68.1 all-reduce.12
  404.2 27.2 reduce-scatter.23
  434.0 28.1 reduce-scatter.25
  464.4 15.2 reduce-scatter.39
  482.1 15.2 reduce-scatter.35
  499.7 15.2 reduce-scatter.37
  517.8 13.1 reduce-scatter.33
  533.7 13.1 reduce-scatter.29
  549.6 13.1 reduce-scatter.27
  565.6 13.1 reduce-scatter.31
  582.4 39.6 all-reduce.16
  624.3 121.4 all-reduce.14
where the time goes:
time: 805 us; the launch traced here: 797 us
  waiting for transfers between devices  392 us (49%)
  matrix products  134 us (17%)
  local copies, waits for them, and re-layouts  104 us (13%)
  blocking collectives  91.8 us (11%)
  other arithmetic  58.1 us (7%)
  between operations  15.8 us (2%)
    psum x1, waiting for transfers between devices, local(): lax.psum(jnp.dot(hidden, down_w, preferred_element_type=jnp.float32).asty...  113 us
    unnamed x22, waiting for transfers between devices  98.9 us
    psum x1, waiting for transfers between devices, local(): lax.psum((jnp.dot(grad_gate, act_w.T, preferred_element_type=jnp.float32)...  58.4 us
    psum x1, waiting for transfers between devices, local(): lax.psum(jnp.dot(mixed_low, out_w, preferred_element_type=jnp.float32).as...  43 us
    unnamed x131, local copies, waits for them, and re-layouts  34.2 us
    psum x1, waiting for transfers between devices, context_total(): lax.psum(query_grad.astype(jnp.bfloat16), 'ctx').astype(jnp.float32)  33.7 us
    psum x1, blocking collectives, local(): lax.psum((gain_first_part, gain_second_grad), ('ctx', 'tp'))  32.3 us
    reduce_scatter x1, waiting for transfers between devices, local(): lax.psum_scatter(value_part.astype(jnp.bfloat16), 'ctx', scatter_dimensio...  24.9 us
  transfers between devices with their start and end apart: 15, of which 14 were waited for; matrix products, arithmetic and copies ran while one was open for 10% of the time, Pallas kernels for 0%

commit v1 on v0

--- a/solution.py
+++ b/solution.py
@@ -340,7 +340,7 @@
         grad_normed_part * gain_first_f, hat_one_part, own_rows(inverse_one)
     )
     gain_first_grad, gain_second_total = lax.psum(
-        (gain_first_part, gain_second_grad), ("ctx", "tp")
+        lax.psum((gain_first_part, gain_second_grad), "tp"), "ctx"
     )
     summed = context_total(query_grad, key_grad, value_grad, act_grad, up_grad, out_grad, down_grad)
     shares = owner_shares(

time: 805 us -> 788 us (0.979)
  blocking collectives: 91.8 us -> 74.8 us
    psum x1 -> x2, blocking collectives: 32.3 us -> 15.4 us  [the longest x1 9.6 us: local(): lax.psum((gain_first_part, gain_second_grad), 'tp')]
where the time goes in v1:
time: 788 us; the launch traced here: 780 us
  waiting for transfers between devices  392 us (50%)
  matrix products  134 us (17%)
  local copies, waits for them, and re-layouts  104 us (13%)
  blocking collectives  74.8 us (9%)
  other arithmetic  58.1 us (7%)
  between operations  15.8 us (2%)
    psum x1, waiting for transfers between devices, local(): lax.psum(jnp.dot(hidden, down_w, preferred_element_type=jnp.float32).asty...  113 us
    unnamed x22, waiting for transfers between devices  98.9 us
    psum x1, waiting for transfers between devices, local(): lax.psum((jnp.dot(grad_gate, act_w.T, preferred_element_type=jnp.float32)...  58.4 us
    psum x1, waiting for transfers between devices, local(): lax.psum(jnp.dot(mixed_low, out_w, preferred_element_type=jnp.float32).as...  43.1 us
    unnamed x131, local copies, waits for them, and re-layouts  34.2 us
    psum x1, waiting for transfers between devices, context_total(): lax.psum(query_grad.astype(jnp.bfloat16), 'ctx').astype(jnp.float32)  33.7 us
    reduce_scatter x1, waiting for transfers between devices, local(): lax.psum_scatter(value_part.astype(jnp.bfloat16), 'ctx', scatter_dimensio...  24.9 us
    dot_general x8, matrix products, per_key(): jnp.einsum('qhd,khd->hqk', grad_block, value_block, preferred_element_typ...  23.3 us
  transfers between devices with their start and end apart: 15, of which 14 were waited for; matrix products, arithmetic and copies ran while one was open for 10% of the time, Pallas kernels for 0%

profile of v1, /device:TPU:0, one launch (start us, length us, event | category | flops | bytes accessed | tf_op | source)
XLA Modules:
  0.0 779.9 jit_solution(5150470857416242544)
XLA Ops:
  8.1 5.2 all-gather
  17.1 5.8 all_gather.37
  26.6 5.8 all_gather.35
  35.4 5.8 all_gather.34
  48.6 6.3 all_gather.39
  54.8 15.1 %all-gather.5.cloned.1.call-done = bf16[4096,192]{0,1:T(8,128)(2,1)} async-done(((bf16[1024,192]{0,1:T(8,128)(2,1)}), bf16[4096,192]{0,1:T(8,128)(2,1)}) %all-gather.5.cloned.1.call-update) | async-done | bytes 1572880 | tf_op jit(solution)/shard_map/all_gather | solution.py:256
  70.0 58.6 %while.42 = (s32[]{:T(128)}, f32[2,512,192]{1,0,2:T(2,128)}, f32[2,512,3]{1,2,0:T(4,128)S(1)}, bf16[2,512,3,64]{1,3,2,0:T(8,128)(2,1)S(1)}, bf16[4096,3,64]{0,2,...) while((s32[]{:T(128)}, f32[2,512,192]{1,0,2:T(2,128)}, f32[2,512,3]{1,2,0:T(4,128)S(1)}, ...), condition=%wide.region_5.6_spmd, body=%wide.region_2.5_spmd.sunk | while | flops 1660956672 | bytes 194132176 | solution.py:82
  70.0 5.0 multiply_reduce_fusion.6
  83.8 10.6 %fusion.155 = f32[3,512,64]{1,2,0:T(8,128)S(1)} fusion(bf16[4096,3,64]{0,2,1:T(8,128)(2,1)S(1)} %copy-done.2, f32[3,512,4096]{2,1,0:T(8,128)} %copy-done, f32[3,512]{1,0:T(4,128)S(1)} %fusion.154), kind=kOutput, calls=%fused_computation.3.clone.1 | convolution fusion | flops 824180736 | bytes 27138048 | tf_op jit(solution)/shard_map/while/body/eval_jaxpr/hqk,khd->qhd/dot_general | solution.py:77
  113.1 10.6 %fusion.155 = f32[3,512,64]{1,2,0:T(8,128)S(1)} fusion(bf16[4096,3,64]{0,2,1:T(8,128)(2,1)S(1)} %copy-done.2, f32[3,512,4096]{2,1,0:T(8,128)} %copy-done, f32[3,512]{1,0:T(4,128)S(1)} %fusion.154), kind=kOutput, calls=%fused_computation.3.clone.1 | convolution fusion | flops 824180736 | bytes 27138048 | tf_op jit(solution)/shard_map/while/body/eval_jaxpr/hqk,khd->qhd/dot_general | solution.py:77
  138.1 7.2 all_gather.41
  145.3 6.7 all_gather.42
  152.0 7.3 all_gather.43
  159.3 43.1 %all-reduce.12.cloned.1.call-done = bf16[1024,768]{1,0:T(8,128)(2,1)} async-done(((bf16[1024,768]{1,0:T(8,128)(2,1)}), bf16[1024,768]{1,0:T(8,128)(2,1)}) %all-reduce.12.cloned.1.call-update) | async-done | bytes 1572880 | tf_op jit(solution)/shard_map/psum | solution.py:263
  225.8 58.4 %all-reduce.14.cloned.1.call-done = bf16[1024,768]{1,0:T(8,128)(2,1)} async-done(((bf16[1024,768]{1,0:T(8,128)(2,1)}), bf16[1024,768]{1,0:T(8,128)(2,1)}) %all-reduce.14.cloned.1.call-update) | async-done | bytes 1572880 | tf_op jit(solution)/shard_map/psum | solution.py:282
  299.2 99.6 %while.44 = (s32[]{:T(128)}, f32[4,1024,3,64]{1,3,2,0:T(8,128)}, f32[4,1024,3,64]{1,3,2,0:T(8,128)}, f32[2,512,3,64]{1,0,3,2:T(2,128)}, bf16[2,512,3,64]{1,3,2,0...) while((s32[]{:T(128)}, f32[4,1024,3,64]{1,3,2,0:T(8,128)}, ...), condition=%wide.region_17.18_spmd, body=%wide.region_14.17_spmd.sunk | while | flops 1021378560 | bytes 39758236 | solution.py:137
  299.2 41.3 %while.45 = (s32[]{:T(128)}, f32[512,3,64]{0,2,1:T(8,128)S(1)}, f32[4,1024,3,64]{1,3,2,0:T(8,128)}, f32[4,1024,3,64]{1,3,2,0:T(8,128)}, bf16[4,1024,3,64]{1,3,2,...) while((s32[]{:T(128)}, f32[512,3,64]{0,2,1:T(8,128)S(1)}, ...), condition=%wide.region_16.16_spmd.clone.clone, body=%wide.region_15.15_spmd.clone.clone.sunk | while | flops 1021378560 | bytes 37374108 | solution.py:131
  340.9 8.1 %dynamic_update_slice.33 = f32[2,512,3,64]{1,0,3,2:T(2,128)} dynamic-update-slice(f32[2,512,3,64]{1,0,3,2:T(2,128)} %get-tuple-element.658, f32[1,512,3,64]{1,0,3,2:T(1,128)S(1)} %copy.87, s32[]{:T(128)S(6)} %copy.120, s32[]{:T(128)} %constant.57.clone.1..sunk.1, s32[]{:T(128)} %constant.57.clone.1..sunk.1, s32[]{:T(128)} %constant.57.clone.1..sunk.1) | dynamic-update-slice | bytes 786436 | tf_op jit(solution)/shard_map/while/body/jit(dynamic_update_index_in_dim)/dynamic_update_slice | solution.py:137
  349.0 41.3 %while.45 = (s32[]{:T(128)}, f32[512,3,64]{0,2,1:T(8,128)S(1)}, f32[4,1024,3,64]{1,3,2,0:T(8,128)}, f32[4,1024,3,64]{1,3,2,0:T(8,128)}, bf16[4,1024,3,64]{1,3,2,...) while((s32[]{:T(128)}, f32[512,3,64]{0,2,1:T(8,128)S(1)}, ...), condition=%wide.region_16.16_spmd.clone.clone, body=%wide.region_15.15_spmd.clone.clone.sunk | while | flops 1021378560 | bytes 37374108 | solution.py:131
  390.7 8.1 %dynamic_update_slice.33 = f32[2,512,3,64]{1,0,3,2:T(2,128)} dynamic-update-slice(f32[2,512,3,64]{1,0,3,2:T(2,128)} %get-tuple-element.658, f32[1,512,3,64]{1,0,3,2:T(1,128)S(1)} %copy.87, s32[]{:T(128)S(6)} %copy.120, s32[]{:T(128)} %constant.57.clone.1..sunk.1, s32[]{:T(128)} %constant.57.clone.1..sunk.1, s32[]{:T(128)} %constant.57.clone.1..sunk.1) | dynamic-update-slice | bytes 786436 | tf_op jit(solution)/shard_map/while/body/jit(dynamic_update_index_in_dim)/dynamic_update_slice | solution.py:137
  437.3 24.9 %reduce-scatter.26.cloned.1.call-done = bf16[1024,192]{0,1:T(8,128)(2,1)} async-done(((bf16[4096,192]{0,1:T(8,128)(2,1)}), bf16[1024,192]{0,1:T(8,128)(2,1)}) %reduce-scatter.26.cloned.1.call-update) | async-done | bytes 393232 | tf_op jit(solution)/shard_map/reduce_scatter | solution.py:309
  467.9 11.8 %reduce-scatter.40.cloned.1.call-done = bf16[384,288]{1,0:T(8,128)(2,1)} async-done(((bf16[768,288]{1,0:T(8,128)(2,1)}), bf16[384,288]{1,0:T(8,128)(2,1)}) %reduce-scatter.40.cloned.1.call-update) | async-done | bytes 221200
  481.5 15.9 %reduce-scatter.36.cloned.1.call-done = bf16[384,288]{1,0:T(8,128)(2,1)} async-done(((bf16[768,288]{1,0:T(8,128)(2,1)}), bf16[384,288]{1,0:T(8,128)(2,1)}) %reduce-scatter.36.cloned.1.call-update) | async-done | bytes 221200
  499.2 15.8 %reduce-scatter.38.cloned.1.call-done = bf16[384,288]{1,0:T(8,128)(2,1)} async-done(((bf16[768,288]{1,0:T(8,128)(2,1)}), bf16[384,288]{1,0:T(8,128)(2,1)}) %reduce-scatter.38.cloned.1.call-update) | async-done | bytes 221200
  516.8 14.1 %reduce-scatter.34.cloned.1.call-done = bf16[384,192]{1,0:T(8,128)(2,1)} async-done(((bf16[768,192]{1,0:T(8,128)(2,1)}), bf16[384,192]{1,0:T(8,128)(2,1)}) %reduce-scatter.34.cloned.1.call-update) | async-done | bytes 147472
  534.3 12.6 %reduce-scatter.30.cloned.1.call-done = bf16[384,192]{1,0:T(8,128)(2,1)} async-done(((bf16[768,192]{1,0:T(8,128)(2,1)}), bf16[384,192]{1,0:T(8,128)(2,1)}) %reduce-scatter.30.cloned.1.call-update) | async-done | bytes 147472
  548.6 14.2 %reduce-scatter.28.cloned.1.call-done = bf16[384,192]{1,0:T(8,128)(2,1)} async-done(((bf16[768,192]{1,0:T(8,128)(2,1)}), bf16[384,192]{1,0:T(8,128)(2,1)}) %reduce-scatter.28.cloned.1.call-update) | async-done | bytes 147472
  564.5 14.3 %reduce-scatter.32.cloned.1.call-done = bf16[384,192]{1,0:T(8,128)(2,1)} async-done(((bf16[768,192]{1,0:T(8,128)(2,1)}), bf16[384,192]{1,0:T(8,128)(2,1)}) %reduce-scatter.32.cloned.1.call-update) | async-done | bytes 147472
  588.4 33.7 %all-reduce.18.cloned.1.call-done = (bf16[384,192]{0,1:T(8,128)(2,1)}, bf16[384,192]{0,1:T(8,128)(2,1)}, bf16[384,192]{0,1:T(8,128)(2,1)}, bf16[192,384]{1,0:T(8...) async-done(((bf16[384,192]{0,1:T(8,128)(2,1)}, bf16[384,192]{0,1:T(8,128)(2,1)}, bf16[384,192]{0,1:T(8,128)(2,1)}, ...) | async-done | bytes 1253392 | tf_op jit(solution)/shard_map/psum | solution.py:196
  633.0 112.9 %all-reduce.16.cloned.1.call-done = (bf16[1024,768]{1,0:T(8,128)(2,1)}, bf16[1024,768]{1,0:T(8,128)(2,1)}) async-done(((bf16[1024,768]{1,0:T(8,128)(2,1)}, bf16[1024,768]{1,0:T(8,128)(2,1)}), (bf16[1024,768]{1,0:T(8,128)(2,1)}, bf16[1024,768]{1,0:T(8,128)(2,1)})) %all-reduce.16.cloned.1.call-update) | async-done | bytes 3145744 | tf_op jit(solution)/shard_map/psum | solution.py:272
  747.2 9.6 %all-reduce.2 = (f32[768]{0:T(1024)S(1)}, f32[768]{0:T(1024)S(1)}) all-reduce(f32[768]{0:T(1024)S(1)} %get-tuple-element.271, f32[768]{0:T(1024)S(1)} %multiply_reduce_fusion.4), channel_id=1, replica_groups=mesh['dp'=2,'ctx'=4,'tp'=4] {'tp'}, use_global_device_ids=true, to_apply=%region_38.39 | all-reduce | flops 1536 | bytes 12288 | tf_op jit(solution)/shard_map/psum | solution.py:343
  756.8 5.8 all-reduce.3
  (344 shorter events, 269.1 us)
Async XLA Ops:
  7.2 15.7 %copy-start.4 = (bf16[1024,768]{1,0:T(8,128)(2,1)S(1)}, bf16[1024,768]{1,0:T(8,128)(2,1)}, u32[]{:S(2)}) copy-start(bf16[1024,768]{1,0:T(8,128)(2,1)} %param.17) | copy-start | bytes 4718596
  7.2 9.8 %copy-start.46 = (bf16[384,192]{0,1:T(8,128)(2,1)S(1)}, bf16[384,192]{0,1:T(8,128)(2,1)}, u32[]{:S(2)}) copy-start(bf16[384,192]{0,1:T(8,128)(2,1)} %param.20) | copy-start | bytes 442372
  7.2 47.6 %all-gather.7.cloned.1.call-start = ((), (), s32[]{:S(2)}) async-start(), calls=%async_computation.10 | async-start | bytes 1966080 | tf_op jit(solution)/shard_map/all_gather | solution.py:257
  13.3 11.8 %copy-start.50 = (f32[768]{0:T(1024)}, f32[768]{0:T(1024)S(1)}, u32[]{:S(2)}) copy-start(f32[768]{0:T(1024)S(1)} %reshape.248) | copy-start | bytes 9220
  25.1 16.1 %copy-start.6 = (bf16[1024,768]{1,0:T(8,128)(2,1)}, bf16[1024,768]{1,0:T(8,128)(2,1)S(1)}, u32[]{:S(2)}) copy-start(bf16[1024,768]{1,0:T(8,128)(2,1)S(1)} %get-tuple-element.358) | copy-start | bytes 4718596
  26.5 43.4 %all-gather.5.cloned.1.call-start = ((), (), s32[]{:S(2)}) async-start(), calls=%async_computation.9 | async-start | bytes 1966080 | tf_op jit(solution)/shard_map/all_gather | solution.py:256
  35.3 167.0 %all-reduce.12.cloned.1.call-start = ((), (), s32[]{:S(2)}) async-start(), calls=%async_computation.11 | async-start | bytes 3145728 | tf_op jit(solution)/shard_map/psum | solution.py:263
  74.9 8.9 %copy-start = (f32[3,512,4096]{2,1,0:T(8,128)}, f32[3,512,4096]{2,1,0:T(8,128)S(1)}, u32[]{:S(2)}) copy-start(f32[3,512,4096]{2,1,0:T(8,128)S(1)} %get-tuple-element.549) | copy-start | bytes 75497472 | tf_op jit(solution)/shard_map/while
  83.8 11.1 %copy-start.36 = (f32[2,512,192]{1,0,2:T(2,128)S(1)}, f32[2,512,192]{1,0,2:T(2,128)}, u32[]{:S(2)}) copy-start(f32[2,512,192]{1,0,2:T(2,128)} %get-tuple-element.626) | copy-start | bytes 2359300 | tf_op jit(solution)/shard_map/while
  113.1 11.0 %copy-start.36 = (f32[2,512,192]{1,0,2:T(2,128)S(1)}, f32[2,512,192]{1,0,2:T(2,128)}, u32[]{:S(2)}) copy-start(f32[2,512,192]{1,0,2:T(2,128)} %get-tuple-element.626) | copy-start | bytes 2359300 | tf_op jit(solution)/shard_map/while
  128.6 9.5 %copy-start.42 = (bf16[384,288]{0,1:T(8,128)(2,1)S(1)}, bf16[384,288]{0,1:T(8,128)(2,1)}, u32[]{:S(2)}) copy-start(bf16[384,288]{0,1:T(8,128)(2,1)} %param.22) | copy-start | bytes 663556
  128.6 16.7 %copy-start.43 = (bf16[384,288]{0,1:T(8,128)(2,1)S(1)}, bf16[384,288]{0,1:T(8,128)(2,1)}, u32[]{:S(2)}) copy-start(bf16[384,288]{0,1:T(8,128)(2,1)} %param.23) | copy-start | bytes 663556
  129.9 74.4 %copy-start.17 = (f32[24,8,2,512]{3,1,2,0:T(8,128)}, f32[24,8,2,512]{3,1,2,0:T(8,128)S(1)}, u32[]{:S(2)}) copy-start(f32[24,8,2,512]{3,1,2,0:T(8,128)S(1)} %copy.80) | copy-start | bytes 2359300
  130.0 22.0 %copy-start.44 = (bf16[288,384]{1,0:T(8,128)(2,1)S(1)}, bf16[288,384]{1,0:T(8,128)(2,1)}, u32[]{:S(2)}) copy-start(bf16[288,384]{1,0:T(8,128)(2,1)} %param.24) | copy-start | bytes 663556
  130.0 72.4 %copy-start.5 = (bf16[1024,768]{1,0:T(8,128)(2,1)S(1)}, bf16[1024,768]{1,0:T(8,128)(2,1)}, u32[]{:S(2)}) copy-start(bf16[1024,768]{1,0:T(8,128)(2,1)} %param.17) | copy-start | bytes 4718596
  133.0 151.2 %all-reduce.14.cloned.1.call-start = ((), (), s32[]{:S(2)}) async-start(), calls=%async_computation.12 | async-start | bytes 3145728 | tf_op jit(solution)/shard_map/psum | solution.py:282
  215.9 215.5 %reduce-scatter.24.cloned.1.call-start = ((), (), s32[]{:S(2)}) async-start(), calls=%async_computation.13 | async-start | bytes 1966080 | tf_op jit(solution)/shard_map/reduce_scatter | solution.py:306
  404.0 58.1 %reduce-scatter.26.cloned.1.call-start = ((), (), s32[]{:S(2)}) async-start(), calls=%async_computation.14 | async-start | bytes 1966080 | tf_op jit(solution)/shard_map/reduce_scatter | solution.py:309
  407.9 71.8 %reduce-scatter.40.cloned.1.call-start = ((), (), s32[]{:S(2)}) async-start(), calls=%async_computation.21 | async-start | bytes 884736
  412.7 84.7 %reduce-scatter.36.cloned.1.call-start = ((), (), s32[]{:S(2)}) async-start(), calls=%async_computation.19 | async-start | bytes 884736
  415.6 99.4 %reduce-scatter.38.cloned.1.call-start = ((), (), s32[]{:S(2)}) async-start(), calls=%async_computation.20 | async-start | bytes 884736
  420.9 110.0 %reduce-scatter.34.cloned.1.call-start = ((), (), s32[]{:S(2)}) async-start(), calls=%async_computation.18 | async-start | bytes 589824
  422.5 8.9 %copy-start.27 = (f32[1024,64]{0,1:T(8,128)S(1)}, f32[1024,64]{0,1:T(8,128)}, u32[]{:S(2)}) copy-start(f32[1024,64]{0,1:T(8,128)} %copy-done.26) | copy-start | bytes 786436
  426.6 120.3 %reduce-scatter.30.cloned.1.call-start = ((), (), s32[]{:S(2)}) async-start(), calls=%async_computation.16 | async-start | bytes 589824
  435.7 127.0 %reduce-scatter.28.cloned.1.call-start = ((), (), s32[]{:S(2)}) async-start(), calls=%async_computation.15 | async-start | bytes 589824
  435.8 28.9 %copy-start.41 = (bf16[288,768]{1,0:T(8,128)(2,1)S(1)}, bf16[288,768]{1,0:T(8,128)(2,1)}, u32[]{:S(2)}) copy-start(bf16[288,768]{1,0:T(8,128)(2,1)} %all_gather.43) | copy-start | bytes 1327108
  437.2 141.5 %reduce-scatter.32.cloned.1.call-start = ((), (), s32[]{:S(2)}) async-start(), calls=%async_computation.17 | async-start | bytes 589824
  464.6 157.5 %all-reduce.18.cloned.1.call-start = ((), (), s32[]{:S(2)}) async-start(), calls=%async_computation.23 | async-start | bytes 2506752 | tf_op jit(solution)/shard_map/psum | solution.py:196
  580.5 165.4 %all-reduce.16.cloned.1.call-start = ((), (), s32[]{:S(2)}) async-start(), calls=%async_computation.22 | async-start | bytes 6291456 | tf_op jit(solution)/shard_map/psum | solution.py:272
  586.8 159.0 %copy-start.19 = (f32[1024,768]{1,0:T(8,128)S(1)}, f32[1024,768]{1,0:T(8,128)}, u32[]{:S(2)}) copy-start(f32[1024,768]{1,0:T(8,128)} %get-tuple-element.357) | copy-start | bytes 9437188
  586.8 159.0 %copy-start.51 = (f32[768]{0:T(1024)S(1)}, f32[768]{0:T(1024)}, u32[]{:S(2)}) copy-start(f32[768]{0:T(1024)} %copy-done.50) | copy-start | bytes 9220
  622.1 10.1 %copy-start.45 = (bf16[288,384]{1,0:T(8,128)(2,1)S(1)}, bf16[288,384]{1,0:T(8,128)(2,1)}, u32[]{:S(2)}) copy-start(bf16[288,384]{1,0:T(8,128)(2,1)} %get-tuple-element.340) | copy-start | bytes 663556
  (46 other events, 137.7 us)
Sparse Core Ops, SparseCore 0:
  26.6 21.4 all-gather.6
  50.3 19.6 all-gather.4
  133.2 69.1 all-reduce.11
  216.0 68.1 all-reduce.13
  404.2 27.2 reduce-scatter.23
  434.0 28.1 reduce-scatter.25
  464.4 15.2 reduce-scatter.39
  482.1 15.2 reduce-scatter.35
  499.7 15.2 reduce-scatter.37
  517.7 13.1 reduce-scatter.33
  533.7 13.1 reduce-scatter.29
  549.6 13.1 reduce-scatter.27
  565.6 13.1 reduce-scatter.31
  582.4 39.6 all-reduce.17
  624.4 121.4 all-reduce.15
